TPU v7x, 32 devices: a whole 2x2x4 slice. The times are simulated.
32 devices in a mesh: parts: 2 (over y), dp: 4 (over z), clu: 2 (over x), sub: 2 (over core).
Axes of the slice: x: 2, y: 2, z: 4, core: 2. Of those that a mesh axis runs over, the one named last changes fastest.
Arguments:
- embeddings: bfloat16 [8192, 4096], P(('parts', 'dp', 'clu'), 'sub'), parts along dimension 0, may hold values from -20 to 20
- projection: bfloat16 [4096, 512], P('sub'), may hold values from -0.09375 to 0.09375
- cluster_ids: int32 [8192], P(('parts', 'dp', 'clu', 'sub')), parts along dimension 0, may hold values from 0 to 7, as said below
Outputs:
- dup_scores: float32 [8192], P(('parts', 'dp', 'clu', 'sub')), parts along dimension 0
There are 2 independent parts, one for each index of `parts`. A program takes and returns all parts, laid end to end along the dimension named above; an argument that names none is the same for every part. Nothing has to cross between parts.
Inputs may be any that keep to these rules, and one draw needn't show every extreme that they name: `cluster_ids`: in each aligned block of 256 rows (the rows of one device) no cluster id appears more than 128 times, and some id appears exactly 128 times.
All inputs are finite; a program needn't handle non-finite values.
Results may differ from a plain program's by a relative error of at most 0.0003.
Values may be sent and summed in bfloat16 or wider, within the bound.
A program may use at most 64 MiB of HBM per device.

v0:
```python
import math

import jax
import jax.numpy as jnp
from jax import lax
from jax.sharding import PartitionSpec as P

sharpness = 10.0
level = 0.5


def pair_weights(queries, key_rows):
    cosine = jnp.einsum("qc,kc->qk", queries, key_rows, preferred_element_type=jnp.float32)
    return jax.nn.sigmoid(sharpness * (cosine - level))


def per_device(embeddings, projection, cluster_ids):
    row_count = cluster_ids.shape[0]
    sketch_width = projection.shape[1]
    owners = lax.axis_size("dp") * lax.axis_size("clu")
    capacity = max(8, 4 * row_count // owners)
    position_count = owners * capacity
    sketch = lax.psum_scatter(
        jnp.dot(embeddings, projection, preferred_element_type=jnp.float32),
        "sub",
        scatter_dimension=0,
        tiled=True,
    )
    scale = lax.rsqrt(jnp.mean(sketch * sketch, axis=1, keepdims=True) + 1e-06) / math.sqrt(
        sketch_width
    )
    unit = (sketch * scale).astype(jnp.bfloat16)
    same_cluster = cluster_ids[:, None] == cluster_ids[None, :]
    row_iota = jnp.arange(row_count, dtype=jnp.int32)
    earlier = row_iota[:, None] > row_iota[None, :]
    slot_rank = jnp.sum((same_cluster & earlier).astype(jnp.int32), axis=1)
    slot_index = cluster_ids * capacity + slot_rank
    outbox = jnp.zeros((position_count, sketch_width), jnp.bfloat16).at[slot_index].set(unit)
    filled = (
        jnp.zeros((position_count,), jnp.bfloat16)
        .at[slot_index]
        .set(jnp.ones((row_count,), jnp.bfloat16))
    )
    inbox, live = (
        lax.all_to_all(
            outbox.reshape(owners, capacity, sketch_width),
            ("dp", "clu"),
            split_axis=0,
            concat_axis=0,
            tiled=True,
        ),
        lax.all_to_all(
            filled.reshape(owners, capacity), ("dp", "clu"), split_axis=0, concat_axis=0, tiled=True
        ),
    )
    inbox = inbox.reshape(position_count, sketch_width)
    core_index = lax.axis_index("sub")
    local_index = jnp.arange(position_count, dtype=jnp.int32)
    block_rows = min(512, position_count)
    own_index = core_index * position_count + local_index
    key_rows = lax.all_gather(inbox, "sub", axis=0, tiled=True)
    key_flags = lax.all_gather(live.reshape(position_count), "sub", axis=0, tiled=True)
    key_index = jnp.arange(key_rows.shape[0], dtype=jnp.int32)
    key_live = key_flags.astype(jnp.float32)

    def one_block(args):
        queries, query_index = args
        weight = pair_weights(queries, key_rows) * key_live[None, :]
        weight = jnp.where(query_index[:, None] == key_index[None, :], jnp.float32(0.0), weight)
        return jnp.sum(weight, axis=1)

    row_sums = lax.map(
        one_block, (inbox.reshape(-1, block_rows, sketch_width), own_index.reshape(-1, block_rows))
    )
    totals = row_sums.reshape(position_count)
    slot_scores = jnp.log1p(totals)
    returned = lax.all_to_all(
        slot_scores.reshape(owners, capacity),
        ("dp", "clu"),
        split_axis=0,
        concat_axis=0,
        tiled=True,
    )
    return returned.reshape(position_count)[slot_index]


def solution(mesh):
    in_specs = (P(("parts", "dp", "clu"), "sub"), P("sub", None), P(("parts", "dp", "clu", "sub")))
    out_specs = P(("parts", "dp", "clu", "sub"))
    return jax.shard_map(
        per_device, mesh=mesh, in_specs=in_specs, out_specs=out_specs, check_vma=False
    )
```

profile of v0, /device:TPU:0, one launch (start us, length us, event | category | flops | bytes accessed | tf_op | source)
XLA Modules:
  0.0 100.6 jit_solution(10938420912099426473)
XLA Ops:
  6.5 0.0 copy-start
  6.5 0.0 copy-start.1
  6.5 0.0 reduce-scatter.2.cloned.1.call-start
  6.5 1.6 %copy-done = bf16[512,2048]{1,0:T(8,128)(2,1)S(1)} copy-done((bf16[512,2048]{1,0:T(8,128)(2,1)S(1)}, bf16[512,2048]{1,0:T(8,128)(2,1)}, u32[]{:S(2)}) %copy-start) | copy-done | bytes 2097176
  8.1 3.8 %fusion.11 = f32[512,512]{1,0:T(8,128)} fusion(bf16[512,2048]{1,0:T(8,128)(2,1)S(1)} %copy-done, bf16[2048,512]{1,0:T(8,128)(2,1)} %param.6), kind=kOutput, calls=%fused_computation.24 | convolution fusion | flops 1073741824 | bytes 5242880 | tf_op jit(solution)/shard_map/dot_general | solution.py:24
  12.0 0.0 reduce-scatter.2.cloned.1.call-update
  12.0 0.0 all-gather.2.cloned.1.call-start
  12.0 0.0 copy-done.1
  12.0 0.2 convert_reduce_fusion
  12.2 11.2 %reduce-scatter.2.cloned.1.call-done = f32[256,512]{1,0:T(8,128)} async-done(((f32[512,512]{1,0:T(8,128)}), f32[256,512]{1,0:T(8,128)}) %reduce-scatter.2.cloned.1.call-update) | async-done | bytes 524304 | tf_op jit(solution)/shard_map/reduce_scatter | solution.py:23
  23.4 1.2 %multiply_reduce_fusion = f32[256]{0:T(256)S(1)} fusion(f32[256,512]{1,0:T(8,128)} %reduce-scatter.2.cloned.1.call-done), kind=kLoop, calls=%fused_computation.11 | loop fusion | flops 261888 | bytes 525312 | tf_op jit(solution)/shard_map/reduce_sum | solution.py:29
  24.6 2.4 %scatter_custom_fusion = bf16[1024,512]{1,0:T(8,128)(2,1)S(1)} fusion(s32[256]{0:T(256)S(1)} %compare_select_fusion, bf16[]{:T(256)} %constant.61.clone.1, f32[256,512]{1,0:T(8,128)} %reduce-scatter.2.cloned.1.call-done, f32[256]{0:T(256)S(1)} %rsqrt_multiply_fusion), kind=kCustom, calls=%fused_computation.12 | custom fusion | flops 262144 | bytes 1573890 | tf_op jit(solution)/shard_map/scatter | solution.py:38
  27.0 31.8 %all_to_all.20 = bf16[8,128,512]{2,1,0:T(8,128)(2,1)} all-to-all(bf16[8,128,512]{2,1,0:T(8,128)(2,1)S(1)} %bitcast.25), channel_id=1, replica_groups=mesh['parts'=2,'dp'=4,'clu'=2,'sub'=2] {'dp','clu'}, dimensions={0} | all-to-all | bytes 2097152 | tf_op jit(solution)/shard_map/all_to_all | solution.py:45
  58.9 0.0 all-gather.2.cloned.1.call-update
  58.9 2.2 %scatter_custom_fusion.1 = bf16[1024]{0:T(1024)(128)(2,1)S(1)} fusion(s32[256]{0:T(256)S(1)} %compare_select_fusion, bf16[256]{0:T(256)(128)(2,1)S(1)} %broadcast.51, bf16[]{:T(256)} %constant.61.clone.1), kind=kCustom, calls=%fused_computation.21 | custom fusion | bytes 2050 | tf_op jit(solution)/shard_map/scatter | solution.py:42
  61.1 0.6 copy.5
  61.7 3.6 %all-to-all-start.1 = ((bf16[8,1,128]{2,1,0:T(2,128)(2,1)}), bf16[8,1,128]{2,1,0:T(2,128)(2,1)S(1)}, u32[]{:S(2)}, u32[]{:S(2)}) async-start(bf16[8,1,128]{2,1,0:T(2,128)(2,1)} %copy.5), calls=%async_computation.2 | async-start | bytes 8192 | tf_op jit(solution)/shard_map/all_to_all | solution.py:52
  65.3 6.4 %all-to-all-done.1 = bf16[8,1,128]{2,1,0:T(2,128)(2,1)S(1)} async-done(((bf16[8,1,128]{2,1,0:T(2,128)(2,1)}), bf16[8,1,128]{2,1,0:T(2,128)(2,1)S(1)}, u32[]{:S(2)}, u32[]{:S(2)}) %all-to-all-start.1) | async-done | bytes 2080 | tf_op jit(solution)/shard_map/all_to_all | solution.py:52
  71.8 1.8 %all_gather.7 = bf16[2048]{0:T(1024)(128)(2,1)S(1)} all-gather(bf16[1024]{0:T(1024)(128)(2,1)S(1)} %bitcast.29), channel_id=1, replica_groups=mesh['parts'=2,'dp'=4,'clu'=2,'sub'=2] {'sub'}, dimensions={0}, use_global_device_ids=true | all-gather | bytes 6144 | tf_op jit(solution)/shard_map/all_gather | solution.py:62
  73.6 0.0 all-gather.2.cloned.1.call-done
  73.6 7.9 %while.13 = (s32[]{:T(128)}, f32[2,512]{1,0:T(2,128)S(1)}, s32[2,512]{1,0:T(2,128)S(1)}, bf16[2,512,512]{2,1,0:T(8,128)(2,1)}, bf16[2048,512]{1,0:T(8,128)(2,1)}, /*index=5*/f32[2048]{0:T(1024)S(1)}, s32[]{:T(128)}, s32[]{:T(128)}) while((s32[]{:T(128)}, f32[2,512]{1,0:T(2,128)S(1)}, s32[2,512]{1,0:T(2,128)S(1)}, ...), condition=%wide.region_7.8_spmd.clone, body=%wide.region_5.7_spmd.clone.sunk | while | flops 1083178496 | bytes 2642525 | solution.py:72
  73.6 3.9 %select_reduce_fusion.2 = f32[512]{0:T(512)S(1)} fusion(bf16[2048,512]{1,0:T(8,128)(2,1)} %get-tuple-element.178, f32[2048]{0:T(1024)S(1)} %get-tuple-element.179, s32[512]{0:T(512)S(1)} %bitcast.27, bf16[2,512,512]{2,1,0:T(8,128)(2,1)} %get-tuple-element.177, s32[]{:T(128)} %get-tuple-element.166), kind=kOutput, calls=%fused_computation.5.clone.1 | convolution fusion | flops 1083178496 | bytes 2634240 | tf_op jit(solution)/shard_map/while/body/eval_jaxpr/qc,kc->qk/dot_general | solution.py:13
  77.6 3.9 %select_reduce_fusion.2 = f32[512]{0:T(512)S(1)} fusion(bf16[2048,512]{1,0:T(8,128)(2,1)} %get-tuple-element.178, f32[2048]{0:T(1024)S(1)} %get-tuple-element.179, s32[512]{0:T(512)S(1)} %bitcast.27, bf16[2,512,512]{2,1,0:T(8,128)(2,1)} %get-tuple-element.177, s32[]{:T(128)} %get-tuple-element.166), kind=kOutput, calls=%fused_computation.5.clone.1 | convolution fusion | flops 1083178496 | bytes 2634240 | tf_op jit(solution)/shard_map/while/body/eval_jaxpr/qc,kc->qk/dot_general | solution.py:13
  81.5 0.6 log1p.15
  82.1 3.3 %all-to-all-start.2 = ((f32[8,1,128]{2,1,0:T(1,128)}), f32[8,1,128]{2,1,0:T(1,128)S(1)}, u32[]{:S(2)}, u32[]{:S(2)}) async-start(f32[8,1,128]{2,1,0:T(1,128)} %log1p.15), calls=%async_computation.3 | async-start | bytes 8192 | tf_op jit(solution)/shard_map/all_to_all | solution.py:77
  85.5 6.4 %all-to-all-done.2 = f32[8,1,128]{2,1,0:T(1,128)S(1)} async-done(((f32[8,1,128]{2,1,0:T(1,128)}), f32[8,1,128]{2,1,0:T(1,128)S(1)}, u32[]{:S(2)}, u32[]{:S(2)}) %all-to-all-start.2) | async-done | bytes 4128 | tf_op jit(solution)/shard_map/all_to_all | solution.py:77
  91.8 1.9 %gather_fusion = f32[256]{0:T(256)} fusion(f32[1024]{0:T(1024)S(1)} %bitcast.22, s32[1024]{0:T(1024)S(1)} %pad_clamp_fusion), kind=kCustom, calls=%fused_computation | custom fusion | bytes 3072 | tf_op jit(solution)/shard_map/gather | solution.py:84
  (13 shorter events, 0.2 us)
Async XLA Ops:
  6.5 1.6 %copy-start = (bf16[512,2048]{1,0:T(8,128)(2,1)S(1)}, bf16[512,2048]{1,0:T(8,128)(2,1)}, u32[]{:S(2)}) copy-start(bf16[512,2048]{1,0:T(8,128)(2,1)} %param.5) | copy-start | bytes 6291460
  6.5 5.5 %copy-start.1 = (s32[256]{0:T(256)S(1)}, s32[256]{0:T(256)}, u32[]{:S(2)}) copy-start(s32[256]{0:T(256)} %param.7) | copy-start | bytes 3076
  6.5 16.8 %reduce-scatter.2.cloned.1.call-start = ((), (), s32[]{:S(2)}) async-start(), calls=%async_computation.4 | async-start | bytes 1572864 | tf_op jit(solution)/shard_map/reduce_scatter | solution.py:23
  12.0 61.6 %all-gather.2.cloned.1.call-start = ((), (), s32[]{:S(2)}) async-start(), calls=%async_computation.5 | async-start | bytes 3145728 | tf_op jit(solution)/shard_map/all_gather | solution.py:61
  61.7 10.1 %all-to-all-start.1 = ((bf16[8,1,128]{2,1,0:T(2,128)(2,1)}), bf16[8,1,128]{2,1,0:T(2,128)(2,1)S(1)}, u32[]{:S(2)}, u32[]{:S(2)}) async-start(bf16[8,1,128]{2,1,0:T(2,128)(2,1)} %copy.5), calls=%async_computation.2 | async-start | bytes 8192 | tf_op jit(solution)/shard_map/all_to_all | solution.py:52
  82.1 9.7 %all-to-all-start.2 = ((f32[8,1,128]{2,1,0:T(1,128)}), f32[8,1,128]{2,1,0:T(1,128)S(1)}, u32[]{:S(2)}, u32[]{:S(2)}) async-start(f32[8,1,128]{2,1,0:T(1,128)} %log1p.15), calls=%async_computation.3 | async-start | bytes 8192 | tf_op jit(solution)/shard_map/all_to_all | solution.py:77
Sparse Core Ops, SparseCore 0:
  12.1 11.2 reduce-scatter.1
  59.0 9.6 all-gather.1
where the time goes:
time: 101 us
  blocking collectives  33.6 us (33%)
  waiting for transfers between devices  24 us (24%)
  between operations  13.5 us (13%)
  matrix products  11.6 us (11%)
  starting transfers between devices  7.01 us (7%)
  local copies, waits for them, and re-layouts  7 us (7%)
  other arithmetic  3.84 us (4%)
    all_to_all x1, blocking collectives, per_device(): lax.all_to_all(outbox.reshape(owners, capacity, sketch_width), ('dp', 'cl...  31.8 us
    reduce_scatter x1, waiting for transfers between devices, per_device(): lax.psum_scatter(jnp.dot(embeddings, projection, preferred_element_type=j...  11.2 us
    dot_general x2, matrix products, pair_weights(): jnp.einsum('qc,kc->qk', queries, key_rows, preferred_element_type=jnp.flo...  7.74 us
    all_to_all x1, waiting for transfers between devices, per_device(): lax.all_to_all(filled.reshape(owners, capacity), ('dp', 'clu'), split_axi...  6.44 us
    all_to_all x1, waiting for transfers between devices, per_device(): lax.all_to_all(slot_scores.reshape(owners, capacity), ('dp', 'clu'), spli...  6.39 us
    dot_general x1, matrix products, per_device(): jnp.dot(embeddings, projection, preferred_element_type=jnp.float32)  3.83 us
    all_to_all x1, starting transfers between devices, per_device(): lax.all_to_all(filled.reshape(owners, capacity), ('dp', 'clu'), split_axi...  3.64 us
    all_to_all x1, starting transfers between devices, per_device(): lax.all_to_all(slot_scores.reshape(owners, capacity), ('dp', 'clu'), spli...  3.33 us
  transfers between devices with their start and end apart: 4, of which 3 were waited for; matrix products, arithmetic and copies ran while one was open for 3% of the time, Pallas kernels for 0%

commit v1 on v0

--- a/solution.py
+++ b/solution.py
@@ -3,10 +3,373 @@
 import jax
 import jax.numpy as jnp
 from jax import lax
+from jax.experimental import pallas as pl
+from jax.experimental.pallas import tpu as pltpu
 from jax.sharding import PartitionSpec as P
 
 sharpness = 10.0
 level = 0.5
+
+MESH = pl.DeviceIdType.MESH
+PARTIAL_CHUNKS = 2
+CHUNKS = 4
+ROUTES = ((1, (2, 3)), (3, (2,)), (0, (1, 2, 3)))
+FIRST, DOWN, LAST = 0, 1, 2
+
+
+def is_any(z, levels):
+    out = z == levels[0]
+    for other in levels[1:]:
+        out = out | (z == other)
+    return out
+
+
+def pair_kernel(
+    emb_ref, proj_ref, ids_ref, out_ref,
+    emb, proj, outgoing, incoming, mine,
+    peers, keys, peer_ids, key_ids, key_cols, own_cols,
+    row_sums, row_recv, key_sums, col_send, col_recv,
+    load_sem, part_send, part_recv, ids_send, ids_recv, kid_send, kid_recv,
+    peer_send, peer_recv, key_send, key_recv, row_ssem, row_rsem, col_ssem, col_rsem,
+):
+    x, z, s = lax.axis_index("clu"), lax.axis_index("dp"), lax.axis_index("sub")
+    rows, width = mine.shape
+    depth = proj.shape[0]
+    target = {
+        1: {"sub": 1 - s},
+        2: {"clu": 1 - x},
+        3: {"clu": 1 - x, "sub": 1 - s},
+    }
+
+    barrier = pltpu.get_barrier_semaphore()
+    for r in (1, 2, 3):
+        pl.semaphore_signal(barrier, inc=1, device_id=target[r], device_id_type=MESH)
+        pl.semaphore_signal(
+            barrier, inc=1, device_id={"dp": lax.rem(z + r, 4)}, device_id_type=MESH
+        )
+
+    half = depth // 2
+    loads = []
+
+    def load(src, dst):
+        copy = pltpu.make_async_copy(src, dst, load_sem.at[len(loads)])
+        copy.start()
+        loads.append(copy)
+
+    peer_rows = pl.ds(pl.multiple_of((1 - s) * rows, rows), rows)
+    own_rows = pl.ds(pl.multiple_of(s * rows, rows), rows)
+    for h in range(2):
+        cut = pl.ds(h * half, half)
+        load(proj_ref.at[cut, :], proj.at[cut, :])
+        load(emb_ref.at[peer_rows, cut], emb.at[0, :, cut])
+    load(emb_ref.at[own_rows, :], emb.at[1])
+
+    ids = jnp.broadcast_to(ids_ref[...].astype(jnp.float32), (8, rows))
+    peer_ids[0] = ids
+
+    def columns(block):
+        return jnp.transpose(jnp.broadcast_to(block[0:1, :], (128, rows)))
+
+    own_cols[...] = columns(ids)
+
+    def remote(src, dst, send, recv, device):
+        return pltpu.make_async_remote_copy(
+            src_ref=src, dst_ref=dst, send_sem=send, recv_sem=recv,
+            device_id=device, device_id_type=MESH,
+        )
+
+    part_rows = rows // PARTIAL_CHUNKS
+
+    def partial(c):
+        cut = pl.ds(c * part_rows, part_rows)
+        return remote(
+            outgoing.at[cut], incoming.at[cut], part_send.at[c], part_recv.at[c], target[1]
+        )
+
+    def ids_copy(r):
+        return remote(peer_ids.at[0], peer_ids.at[r], ids_send.at[r], ids_recv.at[r], target[r])
+
+    def key_ids_copy(k, j):
+        return remote(
+            peer_ids.at[0], key_ids.at[k], kid_send.at[j], kid_recv.at[k],
+            {"dp": ROUTES[k][1][j]},
+        )
+
+    step = rows // CHUNKS
+
+    def peer_copy(r, c):
+        cut = pl.ds(c * step, step)
+        return remote(
+            peers.at[2 if r == 3 else 0, cut], peers.at[r, cut],
+            peer_send.at[r, c], peer_recv.at[r, c], target[2 if r == 2 else 1],
+        )
+
+    def key_copy(k, c, origin):
+        cut = pl.ds(c * step, step)
+        to = z - 1 if k == DOWN else z + 1
+        src = peers.at[0, cut] if origin else keys.at[k, cut]
+        return remote(src, keys.at[k, cut], key_send.at[k, c], key_recv.at[k, c], {"dp": to})
+
+    def rows_copy(r):
+        return remote(row_sums.at[r], row_recv.at[r], row_ssem.at[r], row_rsem.at[r], target[r])
+
+    def cols_copy(k, j):
+        return remote(
+            col_send.at[k], col_recv.at[j], col_ssem.at[k], col_rsem.at[j], {"dp": ROUTES[k][0]}
+        )
+
+    loads[0].wait()
+    loads[1].wait()
+    outgoing[...] = jnp.dot(
+        emb[0, :, 0:half], proj[0:half, :], preferred_element_type=jnp.float32
+    )
+    loads[2].wait()
+    loads[3].wait()
+    pl.semaphore_wait(barrier, 6)
+    for r in (1, 2, 3):
+        ids_copy(r).start()
+    for k, (source, levels) in enumerate(ROUTES):
+
+        @pl.when(z == source)
+        def _():
+            for j in range(len(levels)):
+                key_ids_copy(k, j).start()
+
+    for c in range(PARTIAL_CHUNKS):
+        cut = pl.ds(c * part_rows, part_rows)
+        outgoing[cut, :] += jnp.dot(
+            emb[0, cut, half:depth], proj[half:depth, :], preferred_element_type=jnp.float32
+        )
+        partial(c).start()
+    loads[4].wait()
+    mine[...] = jnp.dot(emb[1], proj[...], preferred_element_type=jnp.float32)
+
+    for c in range(PARTIAL_CHUNKS):
+        cut = pl.ds(c * part_rows, part_rows)
+        partial(c).wait_recv()
+        sketch = mine[cut, :] + incoming[cut, :]
+        scale = lax.rsqrt(
+            jnp.mean(sketch * sketch, axis=1, keepdims=True) + 1e-06
+        ) / math.sqrt(width)
+        peers[0, cut, :] = (sketch * scale).astype(jnp.bfloat16)
+        for d in range(c * CHUNKS // PARTIAL_CHUNKS, (c + 1) * CHUNKS // PARTIAL_CHUNKS):
+            for k, (source, _levels) in enumerate(ROUTES):
+
+                @pl.when(z == source)
+                def _():
+                    key_copy(k, d, True).start()
+
+            peer_copy(2, d).start()
+            peer_copy(1, d).start()
+
+    def double_weights(block, block_cols, r):
+        cosine = lax.dot_general(
+            block, peers[r], (((1,), (1,)), ((), ())), preferred_element_type=jnp.float32
+        )
+        twice = 1.0 + jnp.tanh((0.5 * sharpness) * cosine - (0.5 * sharpness * level))
+        cols = jnp.concatenate([block_cols] * (rows // 128), axis=1)
+        return jnp.where(cols == peer_ids[r, 0:1, :], twice, 0.0)
+
+    def fold_lanes(weights):
+        out = weights[:, 0:128]
+        for t in range(1, rows // 128):
+            out = out + weights[:, t * 128 : (t + 1) * 128]
+        return out
+
+    def fold_rows(weights):
+        return jnp.sum(weights.reshape(weights.shape[0] // 8, 8, weights.shape[1]), axis=0)
+
+    own = double_weights(peers[0], own_cols[...], 0)
+    row_id = lax.broadcasted_iota(jnp.int32, (rows, rows), 0)
+    col_id = lax.broadcasted_iota(jnp.int32, (rows, rows), 1)
+    mine[:, 0:128] = fold_lanes(jnp.where(row_id == col_id, 0.0, own))
+
+    for r in (1, 2, 3):
+        ids_copy(r).wait_recv()
+    for k, (source, levels) in enumerate(ROUTES):
+
+        @pl.when(is_any(z, levels))
+        def _():
+            key_ids_copy(k, 0).wait_recv()
+            key_cols[k] = columns(key_ids[k])
+
+    for c in range(CHUNKS):
+
+        @pl.when(z == 1)
+        def _():
+            key_copy(LAST, c, False).wait_recv()
+            key_copy(LAST, c, False).start()
+
+        @pl.when(z == 2)
+        def _():
+            key_copy(FIRST, c, False).wait_recv()
+            key_copy(FIRST, c, False).start()
+
+        peer_copy(2, c).wait_recv()
+        peer_copy(3, c).start()
+        if c == 0:
+            for d in range(CHUNKS):
+                peer_copy(1, d).wait_recv()
+            mine[:, 0:128] += fold_lanes(double_weights(peers[0], own_cols[...], 1))
+
+    mine[:, 0:128] += fold_lanes(double_weights(peers[0], own_cols[...], 2))
+    for c in range(CHUNKS):
+        peer_copy(3, c).wait_recv()
+    mine[:, 0:128] += fold_lanes(double_weights(peers[0], own_cols[...], 3))
+    out_ref[...] = fold_rows(jnp.transpose(mine[:, 0:128]))
+    row_sums[...] = jnp.zeros_like(row_sums)
+
+    def meet(k, start, count):
+        cut = pl.ds(start, count)
+        block, cols = keys[k, cut, :], key_cols[k, cut, :]
+        total = None
+        for r in range(4):
+            weights = double_weights(block, cols, r)
+            row_sums[r] += fold_rows(weights)
+            lanes = fold_lanes(weights)
+            total = lanes if total is None else total + lanes
+        key_sums[cut, :] = total
+
+    def give_back(k):
+        col_send[k] = fold_rows(jnp.transpose(key_sums[...]))
+        for j, there in enumerate(ROUTES[k][1]):
+
+            @pl.when(z == there)
+            def _():
+                cols_copy(k, j).start()
+
+    @pl.when(z >= 2)
+    def _():
+        @pl.when(z == 3)
+        def _():
+            for c in range(CHUNKS):
+                key_copy(FIRST, c, False).wait_recv()
+
+        meet(FIRST, 0, rows)
+        give_back(FIRST)
+
+    @pl.when(z == 2)
+    def _():
+        for c in range(CHUNKS):
+            key_copy(DOWN, c, False).wait_recv()
+        meet(DOWN, 0, rows)
+        give_back(DOWN)
+
+    @pl.when(z >= 1)
+    def _():
+        for c in range(CHUNKS):
+
+            @pl.when(z >= 2)
+            def _():
+                key_copy(LAST, c, False).wait_recv()
+
+            @pl.when(z == 2)
+            def _():
+                key_copy(LAST, c, False).start()
+
+            meet(LAST, c * step, step)
+        for r in (1, 2, 3):
+            rows_copy(r).start()
+        give_back(LAST)
+        out_ref[...] += row_sums[0]
+        for r in (1, 2, 3):
+            rows_copy(r).wait_recv()
+            out_ref[...] += row_recv[r]
+
+    for k, (source, levels) in enumerate(ROUTES):
+
+        @pl.when(z == source)
+        def _():
+            for j in range(len(levels)):
+                cols_copy(k, j).wait_recv()
+                out_ref[...] += col_recv[j]
+
+    for c in range(PARTIAL_CHUNKS):
+        partial(c).wait_send()
+    for r in (1, 2, 3):
+        ids_copy(r).wait_send()
+        for c in range(CHUNKS):
+            peer_copy(r, c).wait_send()
+
+    @pl.when(z >= 1)
+    def _():
+        for r in (1, 2, 3):
+            rows_copy(r).wait_send()
+
+    for k, (source, levels) in enumerate(ROUTES):
+
+        @pl.when(z == source)
+        def _():
+            for j in range(len(levels)):
+                key_ids_copy(k, j).wait_send()
+
+        @pl.when(is_any(z, (source,) + levels[:-1]))
+        def _():
+            for c in range(CHUNKS):
+                key_copy(k, c, True).wait_send()
+
+        @pl.when(is_any(z, levels))
+        def _():
+            cols_copy(k, 0).wait_send()
+
+
+def all_pairs(embeddings, projection, cluster_ids):
+    rows = cluster_ids.shape[0]
+    depth, width = projection.shape
+    dma = pltpu.SemaphoreType.DMA
+    f32, bf16 = jnp.float32, jnp.bfloat16
+    doubled = pl.pallas_call(
+        pair_kernel,
+        out_shape=jax.ShapeDtypeStruct((8, rows), f32),
+        in_specs=[
+            pl.BlockSpec(memory_space=pl.ANY),
+            pl.BlockSpec(memory_space=pl.ANY),
+            pl.BlockSpec(memory_space=pltpu.VMEM),
+        ],
+        out_specs=pl.BlockSpec(memory_space=pltpu.VMEM),
+        scratch_shapes=[
+            pltpu.VMEM((2, rows, depth), bf16),
+            pltpu.VMEM((depth, width), bf16),
+            pltpu.VMEM((rows, width), f32),
+            pltpu.VMEM((rows, width), f32),
+            pltpu.VMEM((rows, width), f32),
+            pltpu.VMEM((4, rows, width), bf16),
+            pltpu.VMEM((3, rows, width), bf16),
+            pltpu.VMEM((4, 8, rows), f32),
+            pltpu.VMEM((3, 8, rows), f32),
+            pltpu.VMEM((3, rows, 128), f32),
+            pltpu.VMEM((rows, 128), f32),
+            pltpu.VMEM((4, 8, rows), f32),
+            pltpu.VMEM((4, 8, rows), f32),
+            pltpu.VMEM((rows, 128), f32),
+            pltpu.VMEM((3, 8, rows), f32),
+            pltpu.VMEM((3, 8, rows), f32),
+            dma((5,)),
+            dma((PARTIAL_CHUNKS,)),
+            dma((PARTIAL_CHUNKS,)),
+            dma((4,)),
+            dma((4,)),
+            dma((3,)),
+            dma((3,)),
+            dma((4, CHUNKS)),
+            dma((4, CHUNKS)),
+            dma((3, CHUNKS)),
+            dma((3, CHUNKS)),
+            dma((4,)),
+            dma((4,)),
+            dma((3,)),
+            dma((3,)),
+        ],
+        compiler_params=pltpu.CompilerParams(
+            collective_id=0, has_side_effects=True, vmem_limit_bytes=32 * 1024 * 1024
+        ),
+        cost_estimate=pl.CostEstimate(
+            flops=2 * (2 * rows) * depth * width + 2 * 16 * rows * rows * width,
+            bytes_accessed=4 * rows * depth + 2 * depth * width,
+            transcendentals=16 * rows * rows,
+        ),
+    )(embeddings, projection, cluster_ids.reshape(1, rows))
+    return jnp.log1p(0.5 * jnp.sum(doubled, axis=0))
 
 
 def pair_weights(queries, key_rows):
@@ -14,7 +377,7 @@
     return jax.nn.sigmoid(sharpness * (cosine - level))
 
 
-def per_device(embeddings, projection, cluster_ids):
+def routed(embeddings, projection, cluster_ids):
     row_count = cluster_ids.shape[0]
     sketch_width = projection.shape[1]
     owners = lax.axis_size("dp") * lax.axis_size("clu")
@@ -87,6 +450,8 @@
 def solution(mesh):
     in_specs = (P(("parts", "dp", "clu"), "sub"), P("sub", None), P(("parts", "dp", "clu", "sub")))
     out_specs = P(("parts", "dp", "clu", "sub"))
+    sizes = tuple(mesh.shape[name] for name in ("dp", "clu", "sub"))
+    per_device = all_pairs if sizes == (4, 2, 2) else routed
     return jax.shard_map(
         per_device, mesh=mesh, in_specs=in_specs, out_specs=out_specs, check_vma=False
     )

time: 101 us -> 34.4 us (0.34)
  blocking collectives: 33.6 us -> 0 us
  Pallas kernels: 0 us -> 29.7 us
  waiting for transfers between devices: 24 us -> 0 us
  between operations: 13.5 us -> 0.01 us
  matrix products: 11.6 us -> 0 us
  starting transfers between devices: 7.01 us -> 0 us
  other arithmetic: 3.84 us -> 0.59 us
  local copies, waits for them, and re-layouts: 7 us -> 3.86 us
    all_to_all x1 -> x0, blocking collectives: 31.8 us -> none  [per_device(): lax.all_to_all(outbox.reshape(owners, capacity, sketch_width), ('dp', 'cl...]
    pallas_call x0 -> x1, Pallas kernels: none -> 29.7 us  [all_pairs(): pl.pallas_call(pair_kernel, out_shape=jax.ShapeDtypeStruct((8, rows), f32...]
    all_to_all x2 -> x0, waiting for transfers between devices: 12.8 us -> none  [the longest x1 6.44 us: per_device(): lax.all_to_all(filled.reshape(owners, capacity), ('dp', 'clu'), split_axi...]
    dot_general x3 -> x0, matrix products: 11.6 us -> none  [the longest x2 7.74 us: pair_weights(): jnp.einsum('qc,kc->qk', queries, key_rows, preferred_element_type=jnp.flo...]
    reduce_scatter x1 -> x0, waiting for transfers between devices: 11.2 us -> none  [per_device(): lax.psum_scatter(jnp.dot(embeddings, projection, preferred_element_type=j...]
    all_to_all x2 -> x0, starting transfers between devices: 6.97 us -> none  [the longest x1 3.64 us: per_device(): lax.all_to_all(filled.reshape(owners, capacity), ('dp', 'clu'), split_axi...]
    scatter x1 -> x0, other arithmetic: 2.45 us -> none  [per_device(): jnp.zeros((position_count, sketch_width), jnp.bfloat16).at[slot_index]]
    unnamed x4 -> x6, local copies, waits for them, and re-layouts: 1.59 us -> 3.86 us
  transfers between devices with their start and end apart: 4 -> 0, of which waited for: 3 -> 0; matrix products, arithmetic and copies ran while one was open for 3% -> 0% of each run, Pallas kernels for 0% -> 0%
where the time goes in v1:
time: 34.4 us; the launch traced here: 34.2 us
  Pallas kernels  29.7 us (86%)
  local copies, waits for them, and re-layouts  3.86 us (11%)
  other arithmetic  0.59 us (2%)
    pallas_call x1, Pallas kernels, all_pairs(): pl.pallas_call(pair_kernel, out_shape=jax.ShapeDtypeStruct((8, rows), f32...  29.7 us
    unnamed x6, local copies, waits for them, and re-layouts  3.86 us

profile of v1, /device:TPU:0, one launch (start us, length us, event | category | flops | bytes accessed | tf_op | source)
XLA Modules:
  0.0 34.2 jit_solution(3328089432909284866)
XLA Ops:
  0.0 0.0 copy-start
  0.0 1.6 %copy-done = bf16[512,2048]{1,0:T(8,128)(2,1)S(1)} copy-done((bf16[512,2048]{1,0:T(8,128)(2,1)S(1)}, bf16[512,2048]{1,0:T(8,128)(2,1)}, u32[]{:S(2)}) %copy-start) | copy-done | bytes 2097176
  1.6 0.0 copy-start.1
  1.6 1.6 %copy-done.1 = bf16[2048,512]{1,0:T(8,128)(2,1)S(1)} copy-done((bf16[2048,512]{1,0:T(8,128)(2,1)S(1)}, bf16[2048,512]{1,0:T(8,128)(2,1)}, u32[]{:S(2)}) %copy-start.1) | copy-done | bytes 2097176
  3.2 0.0 copy-start.2
  3.2 0.7 %copy-done.2 = s32[256]{0:T(256)S(1)} copy-done((s32[256]{0:T(256)S(1)}, s32[256]{0:T(256)}, u32[]{:S(2)}) %copy-start.2) | copy-done | bytes 1048
  3.9 29.7 %shard_map.37 = f32[8,256]{1,0:T(8,128)S(1)} custom-call(bf16[512,2048]{1,0:T(8,128)(2,1)S(1)} %copy-done, bf16[2048,512]{1,0:T(8,128)(2,1)S(1)} %copy-done.1, s32[1,256]{1,0:T(1,128)S(1)} %bitcast.1), custom_call_target="tpu_custom_call" | custom-call | flops 2147483648 | bytes 4194304 | tf_op jit(solution)/shard_map/pallas_call | solution.py:321
  33.6 0.6 %multiply_log-plus-one_fusion = f32[256]{0:T(256)} fusion(f32[256]{0:T(256)S(1)} %reduce_sum.9), kind=kLoop, calls=%fused_computation | loop fusion | flops 256 | bytes 2048 | tf_op jit(solution)/shard_map/log1p | solution.py:372
  (1 shorter events, 0.0 us)
Async XLA Ops:
  0.0 1.6 %copy-start = (bf16[512,2048]{1,0:T(8,128)(2,1)S(1)}, bf16[512,2048]{1,0:T(8,128)(2,1)}, u32[]{:S(2)}) copy-start(bf16[512,2048]{1,0:T(8,128)(2,1)} %emb_ref.1) | copy-start | bytes 6291460
  1.6 1.6 %copy-start.1 = (bf16[2048,512]{1,0:T(8,128)(2,1)S(1)}, bf16[2048,512]{1,0:T(8,128)(2,1)}, u32[]{:S(2)}) copy-start(bf16[2048,512]{1,0:T(8,128)(2,1)} %proj_ref.1) | copy-start | bytes 6291460
  3.2 0.7 %copy-start.2 = (s32[256]{0:T(256)S(1)}, s32[256]{0:T(256)}, u32[]{:S(2)}) copy-start(s32[256]{0:T(256)} %param.5) | copy-start | bytes 3076

commit v2 on v1

--- a/solution.py
+++ b/solution.py
@@ -13,6 +13,8 @@
 MESH = pl.DeviceIdType.MESH
 PARTIAL_CHUNKS = 2
 CHUNKS = 4
+DETOUR = (0, 1)
+DIRECT = tuple(c for c in range(CHUNKS) if c not in DETOUR)
 ROUTES = ((1, (2, 3)), (3, (2,)), (0, (1, 2, 3)))
 FIRST, DOWN, LAST = 0, 1, 2
 
@@ -27,12 +29,21 @@
 def pair_kernel(
     emb_ref, proj_ref, ids_ref, out_ref,
     emb, proj, outgoing, incoming, mine,
-    peers, keys, peer_ids, key_ids, key_cols, own_cols,
+    peers, keys, transit, peer_ids, key_ids, key_cols, own_cols, own_total,
     row_sums, row_recv, key_sums, col_send, col_recv,
     load_sem, part_send, part_recv, ids_send, ids_recv, kid_send, kid_recv,
     peer_send, peer_recv, key_send, key_recv, row_ssem, row_rsem, col_ssem, col_rsem,
+    way_send, way_recv, home_send,
 ):
-    x, z, s = lax.axis_index("clu"), lax.axis_index("dp"), lax.axis_index("sub")
+    x, s, p = lax.axis_index("clu"), lax.axis_index("sub"), lax.axis_index("parts")
+    height = lax.axis_index("dp")
+    up = 1 - 2 * p
+    z = height + p * (3 - 2 * height)
+    partner = {"parts": 1 - p}
+
+    def lane(there):
+        return {"dp": there + p * (3 - 2 * there)}
+
     rows, width = mine.shape
     depth = proj.shape[0]
     target = {
@@ -45,8 +56,9 @@
     for r in (1, 2, 3):
         pl.semaphore_signal(barrier, inc=1, device_id=target[r], device_id_type=MESH)
         pl.semaphore_signal(
-            barrier, inc=1, device_id={"dp": lax.rem(z + r, 4)}, device_id_type=MESH
-        )
+            barrier, inc=1, device_id={"dp": lax.rem(height + r, 4)}, device_id_type=MESH
+        )
+    pl.semaphore_signal(barrier, inc=1, device_id=partner, device_id_type=MESH)
 
     half = depth // 2
     loads = []
@@ -92,7 +104,7 @@
     def key_ids_copy(k, j):
         return remote(
             peer_ids.at[0], key_ids.at[k], kid_send.at[j], kid_recv.at[k],
-            {"dp": ROUTES[k][1][j]},
+            lane(ROUTES[k][1][j]),
         )
 
     step = rows // CHUNKS
@@ -106,16 +118,29 @@
 
     def key_copy(k, c, origin):
         cut = pl.ds(c * step, step)
-        to = z - 1 if k == DOWN else z + 1
+        to = height - up if k == DOWN else height + up
         src = peers.at[0, cut] if origin else keys.at[k, cut]
         return remote(src, keys.at[k, cut], key_send.at[k, c], key_recv.at[k, c], {"dp": to})
 
+    def way_copy(c, out):
+        cut = pl.ds(c * step, step)
+        return remote(
+            peers.at[0, cut] if out else transit.at[cut], transit.at[cut],
+            way_send.at[0 if out else 1, c], way_recv.at[c], partner if out else {"dp": height - up},
+        )
+
+    def home_copy(c):
+        cut = pl.ds(c * step, step)
+        return remote(
+            transit.at[cut], keys.at[FIRST, cut], home_send.at[c], key_recv.at[FIRST, c], partner
+        )
+
     def rows_copy(r):
         return remote(row_sums.at[r], row_recv.at[r], row_ssem.at[r], row_rsem.at[r], target[r])
 
     def cols_copy(k, j):
         return remote(
-            col_send.at[k], col_recv.at[j], col_ssem.at[k], col_rsem.at[j], {"dp": ROUTES[k][0]}
+            col_send.at[k], col_recv.at[j], col_ssem.at[k], col_rsem.at[j], lane(ROUTES[k][0])
         )
 
     loads[0].wait()
@@ -125,22 +150,22 @@
     )
     loads[2].wait()
     loads[3].wait()
-    pl.semaphore_wait(barrier, 6)
-    for r in (1, 2, 3):
-        ids_copy(r).start()
-    for k, (source, levels) in enumerate(ROUTES):
-
-        @pl.when(z == source)
-        def _():
-            for j in range(len(levels)):
-                key_ids_copy(k, j).start()
-
+    pl.semaphore_wait(barrier, 7)
     for c in range(PARTIAL_CHUNKS):
         cut = pl.ds(c * part_rows, part_rows)
         outgoing[cut, :] += jnp.dot(
             emb[0, cut, half:depth], proj[half:depth, :], preferred_element_type=jnp.float32
         )
         partial(c).start()
+    for r in (1, 2, 3):
+        ids_copy(r).start()
+    for k, (source, levels) in enumerate(ROUTES):
+
+        @pl.when(z == source)
+        def _():
+            for j in range(len(levels)):
+                key_ids_copy(k, j).start()
+
     loads[4].wait()
     mine[...] = jnp.dot(emb[1], proj[...], preferred_element_type=jnp.float32)
 
@@ -157,7 +182,10 @@
 
                 @pl.when(z == source)
                 def _():
-                    key_copy(k, d, True).start()
+                    if k == FIRST and d in DETOUR:
+                        way_copy(d, True).start()
+                    else:
+                        key_copy(k, d, True).start()
 
             peer_copy(2, d).start()
             peer_copy(1, d).start()
@@ -179,19 +207,25 @@
     def fold_rows(weights):
         return jnp.sum(weights.reshape(weights.shape[0] // 8, 8, weights.shape[1]), axis=0)
 
-    own = double_weights(peers[0], own_cols[...], 0)
-    row_id = lax.broadcasted_iota(jnp.int32, (rows, rows), 0)
-    col_id = lax.broadcasted_iota(jnp.int32, (rows, rows), 1)
-    mine[:, 0:128] = fold_lanes(jnp.where(row_id == col_id, 0.0, own))
-
-    for r in (1, 2, 3):
-        ids_copy(r).wait_recv()
-    for k, (source, levels) in enumerate(ROUTES):
-
-        @pl.when(is_any(z, levels))
-        def _():
-            key_ids_copy(k, 0).wait_recv()
-            key_cols[k] = columns(key_ids[k])
+    def own_pairs(r):
+        weights = double_weights(peers[0], own_cols[...], r)
+        if r == 0:
+            row_id = lax.broadcasted_iota(jnp.int32, (rows, rows), 0)
+            col_id = lax.broadcasted_iota(jnp.int32, (rows, rows), 1)
+            mine[:, 0:128] = fold_lanes(jnp.where(row_id == col_id, 0.0, weights))
+        else:
+            mine[:, 0:128] += fold_lanes(weights)
+
+    def pass_transit(c):
+        way_copy(c, False).wait_recv()
+
+        @pl.when(z >= 1)
+        def _():
+            way_copy(c, False).start()
+
+        @pl.when(z <= 1)
+        def _():
+            home_copy(c).start()
 
     for c in range(CHUNKS):
 
@@ -200,23 +234,53 @@
             key_copy(LAST, c, False).wait_recv()
             key_copy(LAST, c, False).start()
 
-        @pl.when(z == 2)
-        def _():
-            key_copy(FIRST, c, False).wait_recv()
-            key_copy(FIRST, c, False).start()
+        if c < len(DETOUR):
+
+            @pl.when(z == 2)
+            def _():
+                pass_transit(DETOUR[c])
+
+        if c < len(DIRECT):
+
+            @pl.when(z == 2)
+            def _():
+                key_copy(FIRST, DIRECT[c], False).wait_recv()
+                key_copy(FIRST, DIRECT[c], False).start()
+
+        if 0 <= c - 1 < len(DETOUR):
+
+            @pl.when(z == 1)
+            def _():
+                pass_transit(DETOUR[c - 1])
 
         peer_copy(2, c).wait_recv()
         peer_copy(3, c).start()
         if c == 0:
+            for r in (1, 2, 3):
+                ids_copy(r).wait_recv()
+            own_pairs(0)
+        if c == 1:
             for d in range(CHUNKS):
                 peer_copy(1, d).wait_recv()
-            mine[:, 0:128] += fold_lanes(double_weights(peers[0], own_cols[...], 1))
-
-    mine[:, 0:128] += fold_lanes(double_weights(peers[0], own_cols[...], 2))
+            own_pairs(1)
+
+    @pl.when(z == 0)
+    def _():
+        for c in DETOUR:
+            pass_transit(c)
+
+    for k, (source, levels) in enumerate(ROUTES):
+
+        @pl.when(is_any(z, levels))
+        def _():
+            key_ids_copy(k, 0).wait_recv()
+            key_cols[k] = columns(key_ids[k])
+
+    own_pairs(2)
     for c in range(CHUNKS):
         peer_copy(3, c).wait_recv()
-    mine[:, 0:128] += fold_lanes(double_weights(peers[0], own_cols[...], 3))
-    out_ref[...] = fold_rows(jnp.transpose(mine[:, 0:128]))
+    own_pairs(3)
+    own_total[...] = fold_rows(jnp.transpose(mine[:, 0:128]))
     row_sums[...] = jnp.zeros_like(row_sums)
 
     def meet(k, start, count):
@@ -228,10 +292,10 @@
             row_sums[r] += fold_rows(weights)
             lanes = fold_lanes(weights)
             total = lanes if total is None else total + lanes
-        key_sums[cut, :] = total
+        key_sums[k, cut, :] = total
 
     def give_back(k):
-        col_send[k] = fold_rows(jnp.transpose(key_sums[...]))
+        col_send[k] = fold_rows(jnp.transpose(key_sums[k]))
         for j, there in enumerate(ROUTES[k][1]):
 
             @pl.when(z == there)
@@ -240,13 +304,13 @@
 
     @pl.when(z >= 2)
     def _():
-        @pl.when(z == 3)
-        def _():
-            for c in range(CHUNKS):
+        for c in DIRECT:
+
+            @pl.when(z == 3)
+            def _():
                 key_copy(FIRST, c, False).wait_recv()
 
-        meet(FIRST, 0, rows)
-        give_back(FIRST)
+            meet(FIRST, c * step, step)
 
     @pl.when(z == 2)
     def _():
@@ -268,13 +332,23 @@
                 key_copy(LAST, c, False).start()
 
             meet(LAST, c * step, step)
+            if 0 <= c - 1 < len(DETOUR):
+                d = DETOUR[c - 1]
+
+                @pl.when(z >= 2)
+                def _():
+                    home_copy(d).wait_recv()
+                    meet(FIRST, d * step, step)
+                    if d == DETOUR[-1]:
+                        give_back(FIRST)
+
         for r in (1, 2, 3):
             rows_copy(r).start()
         give_back(LAST)
-        out_ref[...] += row_sums[0]
+        own_total[...] += row_sums[0]
         for r in (1, 2, 3):
             rows_copy(r).wait_recv()
-            out_ref[...] += row_recv[r]
+            own_total[...] += row_recv[r]
 
     for k, (source, levels) in enumerate(ROUTES):
 
@@ -282,7 +356,9 @@
         def _():
             for j in range(len(levels)):
                 cols_copy(k, j).wait_recv()
-                out_ref[...] += col_recv[j]
+                own_total[...] += col_recv[j]
+
+    out_ref[...] = jnp.sum(own_total[...], axis=0, keepdims=True)
 
     for c in range(PARTIAL_CHUNKS):
         partial(c).wait_send()
@@ -305,12 +381,26 @@
 
         @pl.when(is_any(z, (source,) + levels[:-1]))
         def _():
-            for c in range(CHUNKS):
+            for c in DIRECT if k == FIRST else range(CHUNKS):
                 key_copy(k, c, True).wait_send()
 
         @pl.when(is_any(z, levels))
         def _():
             cols_copy(k, 0).wait_send()
+
+    for c in DETOUR:
+
+        @pl.when(z == 1)
+        def _():
+            way_copy(c, True).wait_send()
+
+        @pl.when(is_any(z, (1, 2)))
+        def _():
+            way_copy(c, False).wait_send()
+
+        @pl.when(z <= 1)
+        def _():
+            home_copy(c).wait_send()
 
 
 def all_pairs(embeddings, projection, cluster_ids):
@@ -320,7 +410,7 @@
     f32, bf16 = jnp.float32, jnp.bfloat16
     doubled = pl.pallas_call(
         pair_kernel,
-        out_shape=jax.ShapeDtypeStruct((8, rows), f32),
+        out_shape=jax.ShapeDtypeStruct((1, rows), f32),
         in_specs=[
             pl.BlockSpec(memory_space=pl.ANY),
             pl.BlockSpec(memory_space=pl.ANY),
@@ -335,13 +425,15 @@
             pltpu.VMEM((rows, width), f32),
             pltpu.VMEM((4, rows, width), bf16),
             pltpu.VMEM((3, rows, width), bf16),
+            pltpu.VMEM((rows, width), bf16),
             pltpu.VMEM((4, 8, rows), f32),
             pltpu.VMEM((3, 8, rows), f32),
             pltpu.VMEM((3, rows, 128), f32),
             pltpu.VMEM((rows, 128), f32),
+            pltpu.VMEM((8, rows), f32),
             pltpu.VMEM((4, 8, rows), f32),
             pltpu.VMEM((4, 8, rows), f32),
-            pltpu.VMEM((rows, 128), f32),
+            pltpu.VMEM((3, rows, 128), f32),
             pltpu.VMEM((3, 8, rows), f32),
             pltpu.VMEM((3, 8, rows), f32),
             dma((5,)),
@@ -359,9 +451,12 @@
             dma((4,)),
             dma((3,)),
             dma((3,)),
+            dma((2, CHUNKS)),
+            dma((CHUNKS,)),
+            dma((CHUNKS,)),
         ],
         compiler_params=pltpu.CompilerParams(
-            collective_id=0, has_side_effects=True, vmem_limit_bytes=32 * 1024 * 1024
+            collective_id=0, has_side_effects=True, vmem_limit_bytes=60 * 1024 * 1024
         ),
         cost_estimate=pl.CostEstimate(
             flops=2 * (2 * rows) * depth * width + 2 * 16 * rows * rows * width,
@@ -369,7 +464,7 @@
             transcendentals=16 * rows * rows,
         ),
     )(embeddings, projection, cluster_ids.reshape(1, rows))
-    return jnp.log1p(0.5 * jnp.sum(doubled, axis=0))
+    return jnp.log1p(0.5 * doubled).reshape(rows)
 
 
 def pair_weights(queries, key_rows):

time: 34.4 us -> 33.1 us (0.962)
  local copies, waits for them, and re-layouts: 3.86 us -> 0 us
  Pallas kernels: 29.7 us -> 31.6 us
  other arithmetic: 0.59 us -> 1.25 us
    unnamed x6 -> x0, local copies, waits for them, and re-layouts: 3.86 us -> none
    pallas_call x1, Pallas kernels: 29.7 us -> 31.6 us  [all_pairs(): pl.pallas_call(pair_kernel, out_shape=jax.ShapeDtypeStruct((1, rows), f32...]
    log1p x1, other arithmetic: 0.58 us -> 1.25 us  [all_pairs(): return jnp.log1p(0.5 * doubled).reshape(rows)]
where the time goes in v2:
time: 33.1 us; the launch traced here: 32.9 us
  Pallas kernels  31.6 us (95%)
  other arithmetic  1.25 us (4%)
    pallas_call x1, Pallas kernels, all_pairs(): pl.pallas_call(pair_kernel, out_shape=jax.ShapeDtypeStruct((1, rows), f32...  31.6 us
    log1p x1, other arithmetic, all_pairs(): return jnp.log1p(0.5 * doubled).reshape(rows)  1.25 us

profile of v2, /device:TPU:0, one launch (start us, length us, event | category | flops | bytes accessed | tf_op | source)
XLA Modules:
  0.0 32.9 jit_solution(2385816885805680484)
XLA Ops:
  0.0 31.6 %shard_map.37 = f32[1,256]{1,0:T(1,128)} custom-call(bf16[512,2048]{1,0:T(8,128)(2,1)} %emb_ref.1, bf16[2048,512]{1,0:T(8,128)(2,1)} %proj_ref.1, s32[1,256]{1,0:T(1,128)} %bitcast.2), custom_call_target="tpu_custom_call" | custom-call | flops 2147483648 | bytes 4194304 | tf_op jit(solution)/shard_map/pallas_call | solution.py:411
  31.6 1.3 %multiply_log-plus-one_fusion = f32[1,256]{1,0:T(1,128)} fusion(f32[1,256]{1,0:T(1,128)} %shard_map.37), kind=kLoop, calls=%fused_computation | loop fusion | flops 256 | bytes 2048 | tf_op jit(solution)/shard_map/log1p | solution.py:467

commit v3 on v1

--- a/solution.py
+++ b/solution.py
@@ -27,7 +27,7 @@
 def pair_kernel(
     emb_ref, proj_ref, ids_ref, out_ref,
     emb, proj, outgoing, incoming, mine,
-    peers, keys, peer_ids, key_ids, key_cols, own_cols,
+    peers, keys, peer_ids, key_ids, key_cols, own_cols, total_ref,
     row_sums, row_recv, key_sums, col_send, col_recv,
     load_sem, part_send, part_recv, ids_send, ids_recv, kid_send, kid_recv,
     peer_send, peer_recv, key_send, key_recv, row_ssem, row_rsem, col_ssem, col_rsem,
@@ -216,7 +216,7 @@
     for c in range(CHUNKS):
         peer_copy(3, c).wait_recv()
     mine[:, 0:128] += fold_lanes(double_weights(peers[0], own_cols[...], 3))
-    out_ref[...] = fold_rows(jnp.transpose(mine[:, 0:128]))
+    total_ref[...] = fold_rows(jnp.transpose(mine[:, 0:128]))
     row_sums[...] = jnp.zeros_like(row_sums)
 
     def meet(k, start, count):
@@ -271,10 +271,10 @@
         for r in (1, 2, 3):
             rows_copy(r).start()
         give_back(LAST)
-        out_ref[...] += row_sums[0]
+        total_ref[...] += row_sums[0]
         for r in (1, 2, 3):
             rows_copy(r).wait_recv()
-            out_ref[...] += row_recv[r]
+            total_ref[...] += row_recv[r]
 
     for k, (source, levels) in enumerate(ROUTES):
 
@@ -282,7 +282,9 @@
         def _():
             for j in range(len(levels)):
                 cols_copy(k, j).wait_recv()
-                out_ref[...] += col_recv[j]
+                total_ref[...] += col_recv[j]
+
+    out_ref[...] = jnp.sum(total_ref[...], axis=0, keepdims=True)
 
     for c in range(PARTIAL_CHUNKS):
         partial(c).wait_send()
@@ -320,7 +322,7 @@
     f32, bf16 = jnp.float32, jnp.bfloat16
     doubled = pl.pallas_call(
         pair_kernel,
-        out_shape=jax.ShapeDtypeStruct((8, rows), f32),
+        out_shape=jax.ShapeDtypeStruct((1, rows), f32),
         in_specs=[
             pl.BlockSpec(memory_space=pl.ANY),
             pl.BlockSpec(memory_space=pl.ANY),
@@ -339,6 +341,7 @@
             pltpu.VMEM((3, 8, rows), f32),
             pltpu.VMEM((3, rows, 128), f32),
             pltpu.VMEM((rows, 128), f32),
+            pltpu.VMEM((8, rows), f32),
             pltpu.VMEM((4, 8, rows), f32),
             pltpu.VMEM((4, 8, rows), f32),
             pltpu.VMEM((rows, 128), f32),
@@ -361,7 +364,7 @@
             dma((3,)),
         ],
         compiler_params=pltpu.CompilerParams(
-            collective_id=0, has_side_effects=True, vmem_limit_bytes=32 * 1024 * 1024
+            collective_id=0, has_side_effects=True, vmem_limit_bytes=60 * 1024 * 1024
         ),
         cost_estimate=pl.CostEstimate(
             flops=2 * (2 * rows) * depth * width + 2 * 16 * rows * rows * width,
@@ -369,7 +372,7 @@
             transcendentals=16 * rows * rows,
         ),
     )(embeddings, projection, cluster_ids.reshape(1, rows))
-    return jnp.log1p(0.5 * jnp.sum(doubled, axis=0))
+    return jnp.log1p(0.5 * doubled).reshape(rows)
 
 
 def pair_weights(queries, key_rows):

time: 34.4 us -> 32.6 us (0.948)
  local copies, waits for them, and re-layouts: 3.86 us -> 0 us
  Pallas kernels: 29.7 us -> 31.2 us
  other arithmetic: 0.59 us -> 1.25 us
    unnamed x6 -> x0, local copies, waits for them, and re-layouts: 3.86 us -> none
    pallas_call x1, Pallas kernels: 29.7 us -> 31.2 us  [all_pairs(): pl.pallas_call(pair_kernel, out_shape=jax.ShapeDtypeStruct((1, rows), f32...]
    log1p x1, other arithmetic: 0.58 us -> 1.25 us  [all_pairs(): return jnp.log1p(0.5 * doubled).reshape(rows)]
where the time goes in v3:
time: 32.6 us; the launch traced here: 32.5 us
  Pallas kernels  31.2 us (96%)
  other arithmetic  1.25 us (4%)
    pallas_call x1, Pallas kernels, all_pairs(): pl.pallas_call(pair_kernel, out_shape=jax.ShapeDtypeStruct((1, rows), f32...  31.2 us
    log1p x1, other arithmetic, all_pairs(): return jnp.log1p(0.5 * doubled).reshape(rows)  1.25 us

profile of v3, /device:TPU:0, one launch (start us, length us, event | category | flops | bytes accessed | tf_op | source)
XLA Modules:
  0.0 32.5 jit_solution(4661067635981611308)
XLA Ops:
  0.0 31.2 %shard_map.37 = f32[1,256]{1,0:T(1,128)} custom-call(bf16[512,2048]{1,0:T(8,128)(2,1)} %emb_ref.1, bf16[2048,512]{1,0:T(8,128)(2,1)} %proj_ref.1, s32[1,256]{1,0:T(1,128)} %bitcast.2), custom_call_target="tpu_custom_call" | custom-call | flops 2147483648 | bytes 4194304 | tf_op jit(solution)/shard_map/pallas_call | solution.py:323
  31.2 1.3 %multiply_log-plus-one_fusion = f32[1,256]{1,0:T(1,128)} fusion(f32[1,256]{1,0:T(1,128)} %shard_map.37), kind=kLoop, calls=%fused_computation | loop fusion | flops 256 | bytes 2048 | tf_op jit(solution)/shard_map/log1p | solution.py:375

commit v4 on v3

--- a/solution.py
+++ b/solution.py
@@ -238,36 +238,32 @@
             def _():
                 cols_copy(k, j).start()
 
-    @pl.when(z >= 2)
-    def _():
-        @pl.when(z == 3)
-        def _():
-            for c in range(CHUNKS):
-                key_copy(FIRST, c, False).wait_recv()
-
-        meet(FIRST, 0, rows)
-        give_back(FIRST)
-
     @pl.when(z == 2)
     def _():
         for c in range(CHUNKS):
-            key_copy(DOWN, c, False).wait_recv()
-        meet(DOWN, 0, rows)
-        give_back(DOWN)
+            key_copy(LAST, c, False).wait_recv()
+            key_copy(LAST, c, False).start()
+            if c == CHUNKS // 2 - 1:
+                meet(FIRST, 0, rows)
+                give_back(FIRST)
+            if c == CHUNKS // 2:
+                for d in range(CHUNKS):
+                    key_copy(DOWN, d, False).wait_recv()
+                meet(DOWN, 0, rows)
+                give_back(DOWN)
+
+    @pl.when(z == 3)
+    def _():
+        for c in range(CHUNKS):
+            key_copy(FIRST, c, False).wait_recv()
+        meet(FIRST, 0, rows)
+        give_back(FIRST)
+        for c in range(CHUNKS):
+            key_copy(LAST, c, False).wait_recv()
 
     @pl.when(z >= 1)
     def _():
-        for c in range(CHUNKS):
-
-            @pl.when(z >= 2)
-            def _():
-                key_copy(LAST, c, False).wait_recv()
-
-            @pl.when(z == 2)
-            def _():
-                key_copy(LAST, c, False).start()
-
-            meet(LAST, c * step, step)
+        meet(LAST, 0, rows)
         for r in (1, 2, 3):
             rows_copy(r).start()
         give_back(LAST)

time: 32.6 us -> 31.5 us (0.966)
  Pallas kernels: 31.2 us -> 30 us
    pallas_call x1, Pallas kernels: 31.2 us -> 30 us  [all_pairs(): pl.pallas_call(pair_kernel, out_shape=jax.ShapeDtypeStruct((1, rows), f32...]
where the time goes in v4:
time: 31.5 us; the launch traced here: 31.3 us
  Pallas kernels  30 us (95%)
  other arithmetic  1.25 us (4%)
    pallas_call x1, Pallas kernels, all_pairs(): pl.pallas_call(pair_kernel, out_shape=jax.ShapeDtypeStruct((1, rows), f32...  30 us
    log1p x1, other arithmetic, all_pairs(): return jnp.log1p(0.5 * doubled).reshape(rows)  1.25 us

profile of v4, /device:TPU:0, one launch (start us, length us, event | category | flops | bytes accessed | tf_op | source)
XLA Modules:
  0.0 31.3 jit_solution(11444528568243347218)
XLA Ops:
  0.0 30.0 %shard_map.37 = f32[1,256]{1,0:T(1,128)} custom-call(bf16[512,2048]{1,0:T(8,128)(2,1)} %emb_ref.1, bf16[2048,512]{1,0:T(8,128)(2,1)} %proj_ref.1, s32[1,256]{1,0:T(1,128)} %bitcast.2), custom_call_target="tpu_custom_call" | custom-call | flops 2147483648 | bytes 4194304 | tf_op jit(solution)/shard_map/pallas_call | solution.py:319
  30.0 1.3 %multiply_log-plus-one_fusion = f32[1,256]{1,0:T(1,128)} fusion(f32[1,256]{1,0:T(1,128)} %shard_map.37), kind=kLoop, calls=%fused_computation | loop fusion | flops 256 | bytes 2048 | tf_op jit(solution)/shard_map/log1p | solution.py:371
